TPU v7x, 32 devices: a whole 2x2x4 slice. The times are simulated.
32 devices in a mesh: blk: 16 (over z, y, x), grp: 2 (over core).
Axes of the slice: x: 2, y: 2, z: 4, core: 2. Of those that a mesh axis runs over, the one named last changes fastest.
Arguments:
- samples: float32 [32, 1024], P(None, ('blk', 'grp')), may hold values from 0 to 256
- bounds: int32 [2, 32, 2048], P(None, None, 'blk'), may hold values from 0 to 256, as said below
- spread: float32 [32], replicated, may hold values from 2 to 8
- counts: int32 [2048], P('blk'), may hold values from 0 to 2047
Outputs:
- log_estimate: float32 [2048], P('blk')
- spread_grad: float32 [32], replicated
Inputs may be any that keep to these rules, and one draw needn't show every extreme that they name: For every query and dimension bounds[0] < bounds[1]; each query restricts exactly 3 dimensions to a width of 16 to 48 cells and has bounds 0 and 256 in all others.
All inputs are finite; a program needn't handle non-finite values.
Results may differ from a plain program's by a relative error of at most 0.0003.
Values sent between devices are 32-bit elements; how exact they have to be, the bound alone decides.
No kernel may reach another device: no remote copies, remote signals or barrier semaphores. Data moves between devices by JAX's collectives and lax.ppermute only.
A program may use at most 64 MiB of HBM per device.

v0:
```python
import functools

import jax
import jax.numpy as jnp
from jax import lax
from jax.experimental import pallas as pl
from jax.experimental.pallas import tpu as pltpu
from jax.sharding import PartitionSpec as P

TABLE_ROWS = 1048576
GRID = 256
LIMITED = 3

ROOT_HALF = 0.7071067811865476
LOG2_E = 1.4426950408889634
SLOPE = 0.5641895835477563


def box_terms(low, high):
    low_bell = jnp.exp2((low * low) * -LOG2_E)
    high_bell = jnp.exp2((high * high) * -LOG2_E)
    return lax.erf(high) - lax.erf(low), low * low_bell - high * high_bell


def split(x, parts):
    out = []
    for _ in range(parts - 1):
        head = x.astype(jnp.bfloat16)
        out.append(head)
        x = x - head.astype(jnp.float32)
    return out + [x.astype(jnp.bfloat16)]


def tree_sum(parts):
    while len(parts) > 1:
        parts = [a + b for a, b in zip(parts[::2], parts[1::2])]
    return parts[0]


def load_kernel(
    x_ref, bounds_ref, spread_ref, counts_ref,
    out_ref, held_bounds, held_spread, target_ref,
    held_x, held_counts, sems,
):
    sources = (x_ref, bounds_ref, spread_ref, counts_ref)
    targets = (held_x, held_bounds, held_spread, held_counts)
    copies = [
        pltpu.make_async_copy(source, target, sems.at[i])
        for i, (source, target) in enumerate(zip(sources, targets))
    ]
    for copy in copies:
        copy.start()
    copies[0].wait()
    rows = held_x.shape[0]
    packed = jnp.concatenate([held_x[8 * j : 8 * (j + 1), :] for j in range(rows // 8)], axis=1)
    for peer in range(out_ref.shape[0]):
        out_ref[peer] = packed
    for copy in copies[1:]:
        copy.wait()
    smoothing = 1.0 / TABLE_ROWS
    target_ref[...] = jnp.log(held_counts[...].astype(jnp.float32) / TABLE_ROWS + smoothing)


def terms_kernel(width, blocks_ref, bounds_ref, spread_ref, out_ref):
    dims, queries = bounds_ref.shape[1:]
    count = blocks_ref.shape[0]
    per_piece = 128 // width
    group = min(count, 4 * per_piece)

    low, high = bounds_ref[0], bounds_ref[1]
    limited = (high - low) != GRID
    at = lax.broadcasted_iota(jnp.int32, (dims, queries), 0)
    first = jnp.min(jnp.where(limited, at, dims), axis=0, keepdims=True)
    last = jnp.max(jnp.where(limited, at, -1), axis=0, keepdims=True)
    chosen = [at == first, limited & (at > first) & (at < last), at == last]

    row = lax.broadcasted_iota(jnp.int32, (dims, dims), 0)
    column = lax.broadcasted_iota(jnp.int32, (dims, dims), 1)
    spread = jnp.sum(jnp.where(row == column, spread_ref[...], 0.0), axis=1, keepdims=True)
    unit = ROOT_HALF / spread

    pick = lambda mask, values: jnp.sum(jnp.where(mask, values, 0.0), axis=0, keepdims=True)
    low = low.astype(jnp.float32) * unit
    high = high.astype(jnp.float32) * unit
    low_at = [pick(mask, low) for mask in chosen]
    high_at = [pick(mask, high) for mask in chosen]

    ones = [mask.astype(jnp.float32).astype(jnp.bfloat16) for mask in chosen]
    free = jnp.where(limited, 0.0, 1.0).astype(jnp.bfloat16)
    none = jnp.zeros_like(free)
    right = jnp.concatenate(
        [jnp.concatenate(ones + [none], axis=1)] * 3
        + [jnp.concatenate([none] * LIMITED + [free], axis=1)] * 3,
        axis=0,
    )

    def step(picked, sums):
        others = jnp.exp2(picked[:, LIMITED * queries :])
        mass, slope = [], []
        for k in range(LIMITED):
            points = picked[:, k * queries : (k + 1) * queries]
            m, s = box_terms(low_at[k] - points, high_at[k] - points)
            mass.append(m)
            slope.append(s)
        pair = others * mass[0]
        last_two = pair * mass[1]
        whole = last_two * mass[2]
        return whole, (
            sums[0] + whole,
            sums[1] + (others * mass[1]) * (mass[2] * slope[0]),
            sums[2] + pair * (mass[2] * slope[1]),
            sums[3] + last_two * slope[2],
        )

    def piece(start, totals):
        sums, products = totals[:-1], totals[-1]
        some = [blocks_ref[start + b] for b in range(per_piece)]
        x = unit * jnp.concatenate(
            [
                jnp.concatenate([block[:, width * j : width * (j + 1)] for block in some], axis=1)
                for j in range(dims // 8)
            ],
            axis=0,
        )
        full, slope = box_terms(-x, float(GRID) * unit - x)
        ratio = jnp.concatenate(split(slope / full, 2), axis=0)
        left = jnp.concatenate(split(x, 3) + split(jnp.log(0.5 * full) * LOG2_E, 3), axis=0)
        picked = lax.dot_general(
            left, right, (((0,), (0,)), ((), ())), preferred_element_type=jnp.float32
        )
        inside = []
        for at_row in range(0, per_piece * width, 16):
            whole, sums = step(picked[at_row : at_row + 16], sums)
            inside.append(jnp.concatenate(split(whole, 2), axis=1))
        inside = jnp.concatenate(inside, axis=0)
        products = products + jnp.dot(ratio, inside, preferred_element_type=jnp.float32)
        return (*sums, products)

    def pieces(number, totals):
        for start in range(0, group, per_piece):
            totals = piece(number * group + start, totals)
        return totals

    zero = jnp.zeros((16, queries), jnp.float32)
    totals = (zero,) * (1 + LIMITED) + (jnp.zeros((2 * dims, 2 * queries), jnp.float32),)
    if count == group:
        totals = pieces(0, totals)
    else:
        totals = lax.fori_loop(0, count // group, pieces, totals)
    sums = [jnp.sum(s, axis=0, keepdims=True) for s in totals[:-1]]
    products = totals[-1]
    deriv = products[:dims, :queries] + (products[dims:, :queries] + products[:dims, queries:])
    deriv = jnp.where(limited, 0.0, deriv * (SLOPE / 4))
    for mask, s in zip(chosen, sums[1:]):
        deriv = jnp.where(mask, s * (SLOPE / 4), deriv)
    out_ref[:dims, :] = deriv
    out_ref[dims:, :] = jnp.broadcast_to(sums[0] * 0.125, (8, queries))


def finish_kernel(sample_total, query_total, *refs):
    part_refs, (target_ref, log_ref, share_ref) = refs[:-3], refs[-3:]
    whole = tree_sum([ref[...] for ref in part_refs])
    dims, queries = whole.shape[0] - 8, whole.shape[1]
    smoothing = 1.0 / TABLE_ROWS
    estimate = whole[dims : dims + 1] / sample_total
    log_est = jnp.log(estimate + smoothing)
    log_ref[...] = log_est
    weight = 2.0 * (log_est - target_ref[...]) / (query_total * (estimate + smoothing))
    terms = whole[:dims] * (weight / sample_total)
    terms = jnp.concatenate([terms, jnp.zeros((queries - dims, queries), jnp.float32)], axis=0)
    share = jnp.sum(terms.T, axis=0, keepdims=True)
    for peer in range(share_ref.shape[0]):
        share_ref[peer] = share


def last_kernel(shares_ref, held_log_ref, log_ref, gradient_ref):
    total = tree_sum([shares_ref[peer] for peer in range(shares_ref.shape[0])])
    log_ref[...] = held_log_ref[0]
    gradient_ref[...] = total[0, : gradient_ref.shape[0]]


def everyone(x, axis):
    size = lax.axis_size(axis)
    return [x] + [
        lax.ppermute(x, axis, [(i, i ^ offset) for i in range(size)]) for offset in range(1, size)
    ]


def call(kernel, args, outs, scratch=(), placed=pltpu.VMEM):
    single = len(outs) == 1
    return pl.pallas_call(
        kernel,
        out_shape=outs[0] if single else outs,
        in_specs=[pl.BlockSpec(memory_space=placed)] * len(args),
        out_specs=pl.BlockSpec(memory_space=pltpu.VMEM)
        if single
        else [pl.BlockSpec(memory_space=pltpu.VMEM)] * len(outs),
        scratch_shapes=list(scratch),
        compiler_params=pltpu.CompilerParams(vmem_limit_bytes=32 << 20),
    )(*args)


def shape(*sizes):
    return jax.ShapeDtypeStruct(sizes, jnp.float32)


def on_device(samples, bounds, spread, counts):
    dims, width = samples.shape
    queries = bounds.shape[2]
    blocks, copies = lax.axis_size("blk"), lax.axis_size("grp")
    sample_total = width * blocks * copies
    query_total = queries * blocks

    counts_vector = pltpu.VMEM((1, queries), jnp.int32)
    packed, bounds, spread, target = call(
        load_kernel,
        [
            pltpu.with_memory_space_constraint(array, pltpu.HBM)
            for array in (samples, bounds, spread.reshape(1, dims), counts.reshape(1, queries))
        ],
        [
            pltpu.VMEM((blocks, 8, dims * width // 8), jnp.float32),
            pltpu.VMEM(bounds.shape, bounds.dtype),
            pltpu.VMEM((1, dims), jnp.float32),
            pltpu.VMEM((1, queries), jnp.float32),
        ],
        [pltpu.VMEM((dims, width), jnp.float32), counts_vector, pltpu.SemaphoreType.DMA((4,))],
        placed=pl.ANY,
    )
    def exchange(x, turned):
        groups = [
            [b * copies + (c + turned(b)) % copies for b in reversed(range(blocks))]
            for c in range(copies)
        ]
        return lax.all_to_all(x, ("blk", "grp"), 0, 0, axis_index_groups=groups)

    gathered = exchange(packed, lambda b: 1 - (b & 7).bit_count() % 2)
    part = call(
        functools.partial(terms_kernel, width),
        [gathered, bounds, spread],
        [shape(dims + 8, queries)],
    )
    log_est, share = call(
        functools.partial(finish_kernel, sample_total, query_total),
        everyone(part, "grp") + [target],
        [shape(1, queries), shape(blocks, 1, queries)],
    )
    shares = exchange(share, lambda b: int(b == 0))
    return call(last_kernel, [shares, log_est], [shape(queries), shape(dims)])


def solution(mesh):
    return jax.shard_map(
        on_device,
        mesh=mesh,
        in_specs=(P(None, ("blk", "grp")), P(None, None, "blk"), P(), P("blk")),
        out_specs=(P("blk"), P()),
        check_vma=False,
    )
```

profile of v0, /device:TPU:0, one launch (start us, length us, event | category | flops | bytes accessed | tf_op | source)
XLA Modules:
  0.0 25.1 jit_solution(17165953976482037023)
XLA Ops:
  0.6 0.8 %shard_map.59 = (f32[16,8,128]{2,1,0:T(8,128)S(1)}, s32[2,32,128]{2,1,0:T(8,128)S(1)}, f32[1,32]{1,0:T(1,128)S(1)}, f32[1,128]{1,0:T(1,128)S(1)}) custom-call(f32[32,32]{1,0:T(8,128)} %x_ref.1, s32[2,32,128]{2,1,0:T(8,128)} %bounds_ref.1, f32[1,32]{1,0:T(1,128)} %bitcast.2, s32[1,128]{1,0:T(1,128)} %bitcast.3), custom_call_target="tpu_custom_call" | custom-call | tf_op jit(solution)/shard_map/pallas_call | solution.py:191
  1.5 12.1 %all_to_all.10.blocks_ref = f32[16,8,128]{2,1,0:T(8,128)S(1)} all-to-all(f32[16,8,128]{2,1,0:T(8,128)S(1)} %get-tuple-element.8), channel_id=1, replica_groups={{30,29,27,24,23,20,18,17,14,13,11,8,7,4,2,1},{31,28,26,25,22,21,19,16,1..., dimensions={0} | all-to-all | bytes 131072 | tf_op jit(solution)/shard_map/all_to_all | solution.py:235
  13.6 1.0 %shard_map.60.refs_0_ = f32[40,128]{1,0:T(8,128)S(1)} custom-call(f32[16,8,128]{2,1,0:T(8,128)S(1)} %all_to_all.10.blocks_ref, s32[2,32,128]{2,1,0:T(8,128)S(1)} %get-tuple-element.9.bounds_ref, f32[1,32]{1,0:T(1,128)S(1)} %get-tuple-element.10.spread_ref), custom_call_target="tpu_custom_call" | custom-call | tf_op jit(solution)/shard_map/pallas_call | solution.py:191
  14.6 0.2 collective-permute-start
  14.8 1.1 %collective-permute-done.refs_1_ = f32[40,128]{1,0:T(8,128)S(1)} collective-permute-done((f32[40,128]{1,0:T(8,128)S(1)}, f32[40,128]{1,0:T(8,128)S(1)}, u32[]{:S(2)}, u32[]{:S(2)}) %collective-permute-start) | collective-permute-done | bytes 20512 | tf_op jit(solution)/shard_map/ppermute | solution.py:185
  15.9 0.1 shard_map.61
  16.0 8.6 %all_to_all.11.shares_ref = f32[16,1,128]{2,1,0:T(1,128)S(1)} all-to-all(f32[16,1,128]{2,1,0:T(1,128)S(1)} %get-tuple-element.12), channel_id=1, replica_groups={{30,28,26,24,22,20,18,16,14,12,10,8,6,4,2,1},{31,29,27,25,23,21,19,17,1..., dimensions={0} | all-to-all | bytes 16384 | tf_op jit(solution)/shard_map/all_to_all | solution.py:235
  24.6 0.5 %shard_map.62 = (f32[128]{0:T(128)}, f32[32]{0:T(128)}) custom-call(f32[16,1,128]{2,1,0:T(1,128)S(1)} %all_to_all.11.shares_ref, f32[1,128]{1,0:T(1,128)S(1)} %get-tuple-element.13.held_log_ref), custom_call_target="tpu_custom_call" | custom-call | tf_op jit(solution)/shard_map/pallas_call | solution.py:191
Async XLA Ops:
  14.6 1.3 %collective-permute-start = (f32[40,128]{1,0:T(8,128)S(1)}, f32[40,128]{1,0:T(8,128)S(1)}, u32[]{:S(2)}, u32[]{:S(2)}) collective-permute-start(f32[40,128]{1,0:T(8,128)S(1)} %shard_map.60.refs_0_), channel_id=1, source_target_pairs={{0,1},{1,0},{2,3},{3,2},{4,5},{5,4},{6,7},{7,6},{8,9},{9,8},{10,11... | collective-permute-start | bytes 61448 | tf_op jit(solution)/shard_map/ppermute | solution.py:185
where the time goes:
time: 25.6 us; the launch traced here: 25.1 us
  blocking collectives  20.7 us (81%)
  Pallas kernels  2.49 us (10%)
  waiting for transfers between devices  1.08 us (4%)
  between operations  0.66 us (3%)
    all_to_all x2, blocking collectives, exchange(): return lax.all_to_all(x, ('blk', 'grp'), 0, 0, axis_index_groups=groups)  20.7 us
    pallas_call x4, Pallas kernels, call(): pl.pallas_call(kernel, out_shape=outs[0] if single else outs, in_specs=[p...  2.49 us
    ppermute x1, waiting for transfers between devices, everyone(): lax.ppermute(x, axis, [(i, i ^ offset) for i in range(size)])  1.08 us
  transfers between devices with their start and end apart: 1, of which 1 were waited for; matrix products, arithmetic and copies ran while one was open for 0% of the time, Pallas kernels for 0%

commit v1 on v0

--- a/solution.py
+++ b/solution.py
@@ -229,12 +229,13 @@
     )
     def exchange(x, turned):
         groups = [
-            [b * copies + (c + turned(b)) % copies for b in reversed(range(blocks))]
-            for c in range(copies)
+            [b * copies + (c + (b in turned)) % copies for b in falling] for c in range(copies)
         ]
         return lax.all_to_all(x, ("blk", "grp"), 0, 0, axis_index_groups=groups)
 
-    gathered = exchange(packed, lambda b: 1 - (b & 7).bit_count() % 2)
+    falling = list(reversed(range(blocks)))
+    far = blocks // 5
+    gathered = exchange(packed, [0] + falling[1 : 1 + far])
     part = call(
         functools.partial(terms_kernel, width),
         [gathered, bounds, spread],
@@ -245,7 +246,7 @@
         everyone(part, "grp") + [target],
         [shape(1, queries), shape(blocks, 1, queries)],
     )
-    shares = exchange(share, lambda b: int(b == 0))
+    shares = exchange(share, [0])
     return call(last_kernel, [shares, log_est], [shape(queries), shape(dims)])
 
 

time: 25.6 us -> 25.6 us (level)
  no operation moved by 1% of the time
where the time goes in v1:
time: 25.6 us; the launch traced here: 25.1 us
  blocking collectives  20.7 us (81%)
  Pallas kernels  2.49 us (10%)
  waiting for transfers between devices  1.17 us (5%)
  between operations  0.66 us (3%)
    all_to_all x2, blocking collectives, exchange(): return lax.all_to_all(x, ('blk', 'grp'), 0, 0, axis_index_groups=groups)  20.7 us
    pallas_call x4, Pallas kernels, call(): pl.pallas_call(kernel, out_shape=outs[0] if single else outs, in_specs=[p...  2.49 us
    ppermute x1, waiting for transfers between devices, everyone(): lax.ppermute(x, axis, [(i, i ^ offset) for i in range(size)])  1.17 us
  transfers between devices with their start and end apart: 1, of which 1 were waited for; matrix products, arithmetic and copies ran while one was open for 0% of the time, Pallas kernels for 0%

profile of v1, /device:TPU:0, one launch (start us, length us, event | category | flops | bytes accessed | tf_op | source)
XLA Modules:
  0.0 25.1 jit_solution(16809888133078574591)
XLA Ops:
  0.6 0.8 %shard_map.59 = (f32[16,8,128]{2,1,0:T(8,128)S(1)}, s32[2,32,128]{2,1,0:T(8,128)S(1)}, f32[1,32]{1,0:T(1,128)S(1)}, f32[1,128]{1,0:T(1,128)S(1)}) custom-call(f32[32,32]{1,0:T(8,128)} %x_ref.1, s32[2,32,128]{2,1,0:T(8,128)} %bounds_ref.1, f32[1,32]{1,0:T(1,128)} %bitcast.2, s32[1,128]{1,0:T(1,128)} %bitcast.3), custom_call_target="tpu_custom_call" | custom-call | tf_op jit(solution)/shard_map/pallas_call | solution.py:191
  1.5 12.1 %all_to_all.10.blocks_ref = f32[16,8,128]{2,1,0:T(8,128)S(1)} all-to-all(f32[16,8,128]{2,1,0:T(8,128)S(1)} %get-tuple-element.8), channel_id=1, replica_groups={{30,29,27,25,22,20,18,16,14,12,10,8,6,4,2,1},{31,28,26,24,23,21,19,17,1..., dimensions={0} | all-to-all | bytes 131072 | tf_op jit(solution)/shard_map/all_to_all | solution.py:234
  13.6 1.0 %shard_map.60.refs_0_ = f32[40,128]{1,0:T(8,128)S(1)} custom-call(f32[16,8,128]{2,1,0:T(8,128)S(1)} %all_to_all.10.blocks_ref, s32[2,32,128]{2,1,0:T(8,128)S(1)} %get-tuple-element.9.bounds_ref, f32[1,32]{1,0:T(1,128)S(1)} %get-tuple-element.10.spread_ref), custom_call_target="tpu_custom_call" | custom-call | tf_op jit(solution)/shard_map/pallas_call | solution.py:191
  14.6 0.1 collective-permute-start
  14.7 1.2 %collective-permute-done.refs_1_ = f32[40,128]{1,0:T(8,128)S(1)} collective-permute-done((f32[40,128]{1,0:T(8,128)S(1)}, f32[40,128]{1,0:T(8,128)S(1)}, u32[]{:S(2)}, u32[]{:S(2)}) %collective-permute-start) | collective-permute-done | bytes 20512 | tf_op jit(solution)/shard_map/ppermute | solution.py:185
  15.9 0.1 shard_map.61
  16.0 8.6 %all_to_all.11.shares_ref = f32[16,1,128]{2,1,0:T(1,128)S(1)} all-to-all(f32[16,1,128]{2,1,0:T(1,128)S(1)} %get-tuple-element.12), channel_id=1, replica_groups={{30,28,26,24,22,20,18,16,14,12,10,8,6,4,2,1},{31,29,27,25,23,21,19,17,1..., dimensions={0} | all-to-all | bytes 16384 | tf_op jit(solution)/shard_map/all_to_all | solution.py:234
  24.6 0.5 %shard_map.62 = (f32[128]{0:T(128)}, f32[32]{0:T(128)}) custom-call(f32[16,1,128]{2,1,0:T(1,128)S(1)} %all_to_all.11.shares_ref, f32[1,128]{1,0:T(1,128)S(1)} %get-tuple-element.13.held_log_ref), custom_call_target="tpu_custom_call" | custom-call | tf_op jit(solution)/shard_map/pallas_call | solution.py:191
Async XLA Ops:
  14.6 1.3 %collective-permute-start = (f32[40,128]{1,0:T(8,128)S(1)}, f32[40,128]{1,0:T(8,128)S(1)}, u32[]{:S(2)}, u32[]{:S(2)}) collective-permute-start(f32[40,128]{1,0:T(8,128)S(1)} %shard_map.60.refs_0_), channel_id=1, source_target_pairs={{0,1},{1,0},{2,3},{3,2},{4,5},{5,4},{6,7},{7,6},{8,9},{9,8},{10,11... | collective-permute-start | bytes 61448 | tf_op jit(solution)/shard_map/ppermute | solution.py:185

commit v2 on v0

--- a/solution.py
+++ b/solution.py
@@ -229,12 +229,12 @@
     )
     def exchange(x, turned):
         groups = [
-            [b * copies + (c + turned(b)) % copies for b in reversed(range(blocks))]
+            [b * copies + (c + (b in turned)) % copies for b in reversed(range(blocks))]
             for c in range(copies)
         ]
         return lax.all_to_all(x, ("blk", "grp"), 0, 0, axis_index_groups=groups)
 
-    gathered = exchange(packed, lambda b: 1 - (b & 7).bit_count() % 2)
+    gathered = exchange(packed, [0])
     part = call(
         functools.partial(terms_kernel, width),
         [gathered, bounds, spread],
@@ -245,7 +245,7 @@
         everyone(part, "grp") + [target],
         [shape(1, queries), shape(blocks, 1, queries)],
     )
-    shares = exchange(share, lambda b: int(b == 0))
+    shares = exchange(share, [0, 1, 2, 4])
     return call(last_kernel, [shares, log_est], [shape(queries), shape(dims)])
 
 

time: 25.6 us -> 26 us (1.016)
  starting transfers between devices: 0.18 us -> 1.01 us
    ppermute x1, starting transfers between devices: 0.18 us -> 1.01 us  [everyone(): lax.ppermute(x, axis, [(i, i ^ offset) for i in range(size)])]
where the time goes in v2:
time: 26 us; the launch traced here: 25.7 us
  blocking collectives  20.7 us (80%)
  Pallas kernels  2.49 us (10%)
  starting transfers between devices  1.01 us (4%)
  waiting for transfers between devices  0.84 us (3%)
  between operations  0.66 us (3%)
    all_to_all x2, blocking collectives, exchange(): return lax.all_to_all(x, ('blk', 'grp'), 0, 0, axis_index_groups=groups)  20.7 us
    pallas_call x4, Pallas kernels, call(): pl.pallas_call(kernel, out_shape=outs[0] if single else outs, in_specs=[p...  2.49 us
    ppermute x1, starting transfers between devices, everyone(): lax.ppermute(x, axis, [(i, i ^ offset) for i in range(size)])  1.01 us
    ppermute x1, waiting for transfers between devices, everyone(): lax.ppermute(x, axis, [(i, i ^ offset) for i in range(size)])  0.84 us
  transfers between devices with their start and end apart: 1, of which 1 were waited for; matrix products, arithmetic and copies ran while one was open for 0% of the time, Pallas kernels for 0%

profile of v2, /device:TPU:0, one launch (start us, length us, event | category | flops | bytes accessed | tf_op | source)
XLA Modules:
  0.0 25.7 jit_solution(15741799236706194847)
XLA Ops:
  0.6 0.8 %shard_map.59 = (f32[16,8,128]{2,1,0:T(8,128)S(1)}, s32[2,32,128]{2,1,0:T(8,128)S(1)}, f32[1,32]{1,0:T(1,128)S(1)}, f32[1,128]{1,0:T(1,128)S(1)}) custom-call(f32[32,32]{1,0:T(8,128)} %x_ref.1, s32[2,32,128]{2,1,0:T(8,128)} %bounds_ref.1, f32[1,32]{1,0:T(1,128)} %bitcast.2, s32[1,128]{1,0:T(1,128)} %bitcast.3), custom_call_target="tpu_custom_call" | custom-call | tf_op jit(solution)/shard_map/pallas_call | solution.py:191
  1.5 11.2 %all_to_all.10.blocks_ref = f32[16,8,128]{2,1,0:T(8,128)S(1)} all-to-all(f32[16,8,128]{2,1,0:T(8,128)S(1)} %get-tuple-element.8), channel_id=1, replica_groups={{30,28,26,24,22,20,18,16,14,12,10,8,6,4,2,1},{31,29,27,25,23,21,19,17,1..., dimensions={0} | all-to-all | bytes 131072 | tf_op jit(solution)/shard_map/all_to_all | solution.py:235
  12.7 1.0 %shard_map.60.refs_0_ = f32[40,128]{1,0:T(8,128)S(1)} custom-call(f32[16,8,128]{2,1,0:T(8,128)S(1)} %all_to_all.10.blocks_ref, s32[2,32,128]{2,1,0:T(8,128)S(1)} %get-tuple-element.9.bounds_ref, f32[1,32]{1,0:T(1,128)S(1)} %get-tuple-element.10.spread_ref), custom_call_target="tpu_custom_call" | custom-call | tf_op jit(solution)/shard_map/pallas_call | solution.py:191
  13.7 1.0 %collective-permute-start = (f32[40,128]{1,0:T(8,128)S(1)}, f32[40,128]{1,0:T(8,128)S(1)}, u32[]{:S(2)}, u32[]{:S(2)}) collective-permute-start(f32[40,128]{1,0:T(8,128)S(1)} %shard_map.60.refs_0_), channel_id=1, source_target_pairs={{0,1},{1,0},{2,3},{3,2},{4,5},{5,4},{6,7},{7,6},{8,9},{9,8},{10,11... | collective-permute-start | bytes 61448 | tf_op jit(solution)/shard_map/ppermute | solution.py:185
  14.7 0.8 %collective-permute-done.refs_1_ = f32[40,128]{1,0:T(8,128)S(1)} collective-permute-done((f32[40,128]{1,0:T(8,128)S(1)}, f32[40,128]{1,0:T(8,128)S(1)}, u32[]{:S(2)}, u32[]{:S(2)}) %collective-permute-start) | collective-permute-done | bytes 20512 | tf_op jit(solution)/shard_map/ppermute | solution.py:185
  15.6 0.1 shard_map.61
  15.7 9.5 %all_to_all.11.shares_ref = f32[16,1,128]{2,1,0:T(1,128)S(1)} all-to-all(f32[16,1,128]{2,1,0:T(1,128)S(1)} %get-tuple-element.12), channel_id=1, replica_groups={{30,28,26,24,22,20,18,16,14,12,10,9,6,5,3,1},{31,29,27,25,23,21,19,17,1..., dimensions={0} | all-to-all | bytes 16384 | tf_op jit(solution)/shard_map/all_to_all | solution.py:235
  25.1 0.5 %shard_map.62 = (f32[128]{0:T(128)}, f32[32]{0:T(128)}) custom-call(f32[16,1,128]{2,1,0:T(1,128)S(1)} %all_to_all.11.shares_ref, f32[1,128]{1,0:T(1,128)S(1)} %get-tuple-element.13.held_log_ref), custom_call_target="tpu_custom_call" | custom-call | tf_op jit(solution)/shard_map/pallas_call | solution.py:191
Async XLA Ops:
  13.7 1.9 %collective-permute-start = (f32[40,128]{1,0:T(8,128)S(1)}, f32[40,128]{1,0:T(8,128)S(1)}, u32[]{:S(2)}, u32[]{:S(2)}) collective-permute-start(f32[40,128]{1,0:T(8,128)S(1)} %shard_map.60.refs_0_), channel_id=1, source_target_pairs={{0,1},{1,0},{2,3},{3,2},{4,5},{5,4},{6,7},{7,6},{8,9},{9,8},{10,11... | collective-permute-start | bytes 61448 | tf_op jit(solution)/shard_map/ppermute | solution.py:185

commit v3 on v2

--- a/solution.py
+++ b/solution.py
@@ -245,7 +245,7 @@
         everyone(part, "grp") + [target],
         [shape(1, queries), shape(blocks, 1, queries)],
     )
-    shares = exchange(share, [0, 1, 2, 4])
+    shares = exchange(share, [0] + list(range(blocks // 2, blocks)))
     return call(last_kernel, [shares, log_est], [shape(queries), shape(dims)])
 
 

time: 26 us -> 26.2 us (level)
  no operation moved by 1% of the time
where the time goes in v3:
time: 26.2 us; the launch traced here: 25.9 us
  blocking collectives  20.9 us (80%)
  Pallas kernels  2.49 us (10%)
  starting transfers between devices  1.01 us (4%)
  waiting for transfers between devices  0.84 us (3%)
  between operations  0.66 us (3%)
    all_to_all x2, blocking collectives, exchange(): return lax.all_to_all(x, ('blk', 'grp'), 0, 0, axis_index_groups=groups)  20.9 us
    pallas_call x4, Pallas kernels, call(): pl.pallas_call(kernel, out_shape=outs[0] if single else outs, in_specs=[p...  2.49 us
    ppermute x1, starting transfers between devices, everyone(): lax.ppermute(x, axis, [(i, i ^ offset) for i in range(size)])  1.01 us
    ppermute x1, waiting for transfers between devices, everyone(): lax.ppermute(x, axis, [(i, i ^ offset) for i in range(size)])  0.84 us
  transfers between devices with their start and end apart: 1, of which 1 were waited for; matrix products, arithmetic and copies ran while one was open for 0% of the time, Pallas kernels for 0%

profile of v3, /device:TPU:0, one launch (start us, length us, event | category | flops | bytes accessed | tf_op | source)
XLA Modules:
  0.0 25.9 jit_solution(13484782354777790820)
XLA Ops:
  0.6 0.8 %shard_map.59 = (f32[16,8,128]{2,1,0:T(8,128)S(1)}, s32[2,32,128]{2,1,0:T(8,128)S(1)}, f32[1,32]{1,0:T(1,128)S(1)}, f32[1,128]{1,0:T(1,128)S(1)}) custom-call(f32[32,32]{1,0:T(8,128)} %x_ref.1, s32[2,32,128]{2,1,0:T(8,128)} %bounds_ref.1, f32[1,32]{1,0:T(1,128)} %bitcast.2, s32[1,128]{1,0:T(1,128)} %bitcast.3), custom_call_target="tpu_custom_call" | custom-call | tf_op jit(solution)/shard_map/pallas_call | solution.py:191
  1.5 11.2 %all_to_all.10.blocks_ref = f32[16,8,128]{2,1,0:T(8,128)S(1)} all-to-all(f32[16,8,128]{2,1,0:T(8,128)S(1)} %get-tuple-element.8), channel_id=1, replica_groups={{30,28,26,24,22,20,18,16,14,12,10,8,6,4,2,1},{31,29,27,25,23,21,19,17,1..., dimensions={0} | all-to-all | bytes 131072 | tf_op jit(solution)/shard_map/all_to_all | solution.py:235
  12.7 1.0 %shard_map.60.refs_0_ = f32[40,128]{1,0:T(8,128)S(1)} custom-call(f32[16,8,128]{2,1,0:T(8,128)S(1)} %all_to_all.10.blocks_ref, s32[2,32,128]{2,1,0:T(8,128)S(1)} %get-tuple-element.9.bounds_ref, f32[1,32]{1,0:T(1,128)S(1)} %get-tuple-element.10.spread_ref), custom_call_target="tpu_custom_call" | custom-call | tf_op jit(solution)/shard_map/pallas_call | solution.py:191
  13.7 1.0 %collective-permute-start = (f32[40,128]{1,0:T(8,128)S(1)}, f32[40,128]{1,0:T(8,128)S(1)}, u32[]{:S(2)}, u32[]{:S(2)}) collective-permute-start(f32[40,128]{1,0:T(8,128)S(1)} %shard_map.60.refs_0_), channel_id=1, source_target_pairs={{0,1},{1,0},{2,3},{3,2},{4,5},{5,4},{6,7},{7,6},{8,9},{9,8},{10,11... | collective-permute-start | bytes 61448 | tf_op jit(solution)/shard_map/ppermute | solution.py:185
  14.7 0.8 %collective-permute-done.refs_1_ = f32[40,128]{1,0:T(8,128)S(1)} collective-permute-done((f32[40,128]{1,0:T(8,128)S(1)}, f32[40,128]{1,0:T(8,128)S(1)}, u32[]{:S(2)}, u32[]{:S(2)}) %collective-permute-start) | collective-permute-done | bytes 20512 | tf_op jit(solution)/shard_map/ppermute | solution.py:185
  15.6 0.1 shard_map.61
  15.7 9.7 %all_to_all.11.shares_ref = f32[16,1,128]{2,1,0:T(1,128)S(1)} all-to-all(f32[16,1,128]{2,1,0:T(1,128)S(1)} %get-tuple-element.12), channel_id=1, replica_groups={{31,29,27,25,23,21,19,17,14,12,10,8,6,4,2,1},{30,28,26,24,22,20,18,16,1..., dimensions={0} | all-to-all | bytes 16384 | tf_op jit(solution)/shard_map/all_to_all | solution.py:235
  25.4 0.5 %shard_map.62 = (f32[128]{0:T(128)}, f32[32]{0:T(128)}) custom-call(f32[16,1,128]{2,1,0:T(1,128)S(1)} %all_to_all.11.shares_ref, f32[1,128]{1,0:T(1,128)S(1)} %get-tuple-element.13.held_log_ref), custom_call_target="tpu_custom_call" | custom-call | tf_op jit(solution)/shard_map/pallas_call | solution.py:191
Async XLA Ops:
  13.7 1.9 %collective-permute-start = (f32[40,128]{1,0:T(8,128)S(1)}, f32[40,128]{1,0:T(8,128)S(1)}, u32[]{:S(2)}, u32[]{:S(2)}) collective-permute-start(f32[40,128]{1,0:T(8,128)S(1)} %shard_map.60.refs_0_), channel_id=1, source_target_pairs={{0,1},{1,0},{2,3},{3,2},{4,5},{5,4},{6,7},{7,6},{8,9},{9,8},{10,11... | collective-permute-start | bytes 61448 | tf_op jit(solution)/shard_map/ppermute | solution.py:185
